TPU v7x, 256 devices: a whole 4x4x8 slice. The times are simulated.
256 devices in a mesh: ckpt: 16 (over x, z_hi), tensor: 16 (over z_lo, y, core).
Axes of the slice: x: 4, y: 4, z: 8 (z_hi: 4, z_lo: 2; z = z_hi * 2 + z_lo), core: 2. Of those that a mesh axis runs over, the one named last changes fastest.
Arguments:
- acts: bfloat16 [16, 2048, 3584], P('ckpt', 'tensor'), may hold values from -6 to 6
- cotangent: bfloat16 [16, 2048, 8192], P('ckpt', None, 'tensor'), may hold values from -0.29882812 to 0.29882812
- seq_lengths: int32 [4], replicated, may hold values from 1 to 512, 1536 in all
- up_weight: bfloat16 [16, 3584, 8192], P('ckpt', None, 'tensor'), may hold values from -0.125 to 0.125
Outputs:
- merged: bfloat16 [3584, 8192], P(None, 'tensor')
All inputs are finite; a program needn't handle non-finite values.
Results may differ from a plain program's by a relative error of at most 0.001.
Values may be sent and summed in bfloat16 or wider, within the bound.
A program may use at most 128 MiB of HBM per device.

v0:
```python
import jax
import jax.numpy as jnp
from jax import lax
from jax.sharding import PartitionSpec as P


def body(acts, cotangent, seq_lengths, up_weight):
    all_rows = lax.all_gather(acts[0], "tensor", axis=0, tiled=True)
    grads = cotangent[0]
    seq_count = seq_lengths.shape[0]
    seq_len = grads.shape[0] // seq_count
    width = all_rows.shape[1]
    cols = grads.shape[1]
    positions = jnp.arange(seq_len, dtype=jnp.int32)
    live = positions[None, :] < seq_lengths[:, None]
    shaped_g = grads.reshape(seq_count, seq_len, cols)
    shaped_g = jnp.where(live[:, :, None], shaped_g, jnp.zeros_like(shaped_g))
    shaped_in = all_rows.reshape(seq_count, seq_len, width)

    def one_seq(total, pair):
        x_rows, g_rows = pair
        grad = lax.dot_general(
            x_rows, g_rows, (((0,), (0,)), ((), ())), preferred_element_type=jnp.float32
        )
        return (total + grad * grad, None)

    start = jnp.zeros((width, cols), jnp.float32)
    fisher, unused = lax.scan(one_seq, start, (shaped_in, shaped_g))
    numer = fisher * up_weight[0].astype(jnp.float32)
    numer_part, denom_part = (
        lax.psum_scatter(numer, "ckpt", scatter_dimension=0, tiled=True),
        lax.psum_scatter(fisher, "ckpt", scatter_dimension=0, tiled=True),
    )
    merged_part = (numer_part / (denom_part + 1e-06)).astype(jnp.bfloat16)
    merged = lax.all_gather(merged_part, "ckpt", axis=0, tiled=True)
    return merged


def solution(mesh):
    in_specs = (
        P("ckpt", "tensor", None),
        P("ckpt", None, "tensor"),
        P(),
        P("ckpt", None, "tensor"),
    )
    out_specs = P(None, "tensor")
    return jax.shard_map(body, mesh=mesh, in_specs=in_specs, out_specs=out_specs, check_vma=False)
```

profile of v0, /device:TPU:2, one launch (start us, length us, event | category | flops | bytes accessed | tf_op | source)
XLA Modules:
  0.0 446.3 jit_solution(14538628846678960847)
XLA Ops:
  6.5 0.0 all-gather.6.cloned.1.call-start
  6.5 0.7 all-gather.6.cloned.1.call-update
  7.3 0.0 reduce-scatter.5.cloned.1.call-start
  7.3 0.7 iota_compare_fusion
  8.0 1.8 broadcast_select_fusion
  9.8 86.7 %all-gather.6.cloned.1.call-done = bf16[1,2048,3584]{2,1,0:T(8,128)(2,1)} async-done(((bf16[1,128,3584]{2,1,0:T(8,128)(2,1)}), bf16[1,2048,3584]{2,1,0:T(8,128)(2,1)}) %all-gather.6.cloned.1.call-update) | async-done | bytes 14680080 | tf_op jit(solution)/shard_map/all_gather | solution.py:8
  96.5 34.9 %while.11 = (s32[]{:T(128)}, f32[3584,512]{1,0:T(8,128)}, bf16[4,512,3584]{2,1,0:T(8,128)(2,1)}, bf16[4,512,512]{2,1,0:T(8,128)(2,1)S(1)}, s32[]{:T(128)}, /*index=5*/s32[]{:T(128)}) while((s32[]{:T(128)}, f32[3584,512]{1,0:T(8,128)}, bf16[4,512,3584]{2,1,0:T(8,128)(2,1)}, bf16[4,512,512]{2,1,0:T(8,128)(2,1)S(1)}, s32[]{:T(128)}, ...), condition=%wide.region_1.2_spmd.clone, body=%wide.region_0.1_spmd.clone.sunk | while | flops 1884553216 | bytes 18875988 | solution.py:28
  96.5 7.1 %select_add_fusion.2 = f32[3584,512]{1,0:T(8,128)} fusion(f32[3584,512]{1,0:T(8,128)} %get-tuple-element.83, bf16[4,512,3584]{2,1,0:T(8,128)(2,1)} %get-tuple-element.90, s32[]{:T(128)S(6)} %copy.7, pred[]{:T(512)S(6)} %compare.3, bf16[4,512,512]{2,1,0:T(8,128)(2,1)S(1)} %get-tuple-element.91), kind=kOutput, calls=%fused_computation.1.clone.1 | convolution fusion | flops 1884553216 | bytes 18875904 | tf_op jit(solution)/shard_map/while/body/eval_jaxpr/dot_general | solution.py:22
  103.6 9.3 %select_add_fusion.2 = f32[3584,512]{1,0:T(8,128)} fusion(f32[3584,512]{1,0:T(8,128)} %get-tuple-element.83, bf16[4,512,3584]{2,1,0:T(8,128)(2,1)} %get-tuple-element.90, s32[]{:T(128)S(6)} %copy.7, pred[]{:T(512)S(6)} %compare.3, bf16[4,512,512]{2,1,0:T(8,128)(2,1)S(1)} %get-tuple-element.91), kind=kOutput, calls=%fused_computation.1.clone.1 | convolution fusion | flops 1884553216 | bytes 18875904 | tf_op jit(solution)/shard_map/while/body/eval_jaxpr/dot_general | solution.py:22
  112.9 9.3 %select_add_fusion.2 = f32[3584,512]{1,0:T(8,128)} fusion(f32[3584,512]{1,0:T(8,128)} %get-tuple-element.83, bf16[4,512,3584]{2,1,0:T(8,128)(2,1)} %get-tuple-element.90, s32[]{:T(128)S(6)} %copy.7, pred[]{:T(512)S(6)} %compare.3, bf16[4,512,512]{2,1,0:T(8,128)(2,1)S(1)} %get-tuple-element.91), kind=kOutput, calls=%fused_computation.1.clone.1 | convolution fusion | flops 1884553216 | bytes 18875904 | tf_op jit(solution)/shard_map/while/body/eval_jaxpr/dot_general | solution.py:22
  122.1 9.3 %select_add_fusion.2 = f32[3584,512]{1,0:T(8,128)} fusion(f32[3584,512]{1,0:T(8,128)} %get-tuple-element.83, bf16[4,512,3584]{2,1,0:T(8,128)(2,1)} %get-tuple-element.90, s32[]{:T(128)S(6)} %copy.7, pred[]{:T(512)S(6)} %compare.3, bf16[4,512,512]{2,1,0:T(8,128)(2,1)S(1)} %get-tuple-element.91), kind=kOutput, calls=%fused_computation.1.clone.1 | convolution fusion | flops 1884553216 | bytes 18875904 | tf_op jit(solution)/shard_map/while/body/eval_jaxpr/dot_general | solution.py:22
  131.4 0.0 reduce-scatter.5.cloned.1.call-update
  131.4 0.0 reduce-scatter.3.cloned.1.call-start
  131.5 8.2 %convert_multiply_fusion = f32[3584,512]{1,0:T(8,128)} fusion(f32[3584,512]{1,0:T(8,128)} %get-tuple-element.27, bf16[1,3584,512]{2,1,0:T(8,128)(2,1)} %param.9), kind=kLoop, calls=%fused_computation.7 | loop fusion | flops 3670016 | bytes 18350080 | tf_op jit(solution)/shard_map/mul | solution.py:29
  139.7 0.0 reduce-scatter.3.cloned.1.call-update
  139.7 0.0 all-gather.4.cloned.1.call-start
  139.8 107.1 %reduce-scatter.5.cloned.1.call-done = f32[224,512]{1,0:T(8,128)} async-done(((f32[3584,512]{1,0:T(8,128)}), f32[224,512]{1,0:T(8,128)}) %reduce-scatter.5.cloned.1.call-update) | async-done | bytes 458768 | tf_op jit(solution)/shard_map/reduce_scatter | solution.py:32
  246.9 116.3 %reduce-scatter.3.cloned.1.call-done = f32[224,512]{1,0:T(8,128)} async-done(((f32[3584,512]{1,0:T(8,128)}), f32[224,512]{1,0:T(8,128)}) %reduce-scatter.3.cloned.1.call-update) | async-done | bytes 458768 | tf_op jit(solution)/shard_map/reduce_scatter | solution.py:31
  363.2 1.9 divide_convert_fusion
  365.1 0.0 all-gather.4.cloned.1.call-update
  365.1 70.5 %all-gather.4.cloned.1.call-done = bf16[3584,512]{1,0:T(8,128)(2,1)} async-done(((bf16[224,512]{1,0:T(8,128)(2,1)}), bf16[3584,512]{1,0:T(8,128)(2,1)}) %all-gather.4.cloned.1.call-update) | async-done | bytes 3670032 | tf_op jit(solution)/shard_map/all_gather | solution.py:35
  435.7 4.1 copy.12
  (1 shorter events, 0.0 us)
Async XLA Ops:
  6.5 90.0 %all-gather.6.cloned.1.call-start = ((), (), s32[]{:S(2)}) async-start(), calls=%async_computation.5 | async-start | bytes 15597568 | tf_op jit(solution)/shard_map/all_gather | solution.py:8
  7.3 239.7 %reduce-scatter.5.cloned.1.call-start = ((), (), s32[]{:S(2)}) async-start(), calls=%async_computation.3 | async-start | bytes 7798784 | tf_op jit(solution)/shard_map/reduce_scatter | solution.py:32
  131.4 231.8 %reduce-scatter.3.cloned.1.call-start = ((), (), s32[]{:S(2)}) async-start(), calls=%async_computation.2 | async-start | bytes 7798784 | tf_op jit(solution)/shard_map/reduce_scatter | solution.py:31
  139.7 296.0 %all-gather.4.cloned.1.call-start = ((), (), s32[]{:S(2)}) async-start(), calls=%async_computation.4 | async-start | bytes 3899392 | tf_op jit(solution)/shard_map/all_gather | solution.py:35
Sparse Core Ops, SparseCore 0:
  9.2 87.2 all-gather.5
  131.5 115.3 reduce-scatter.4
  251.2 111.9 reduce-scatter.2
  365.5 70.1 all-gather.3
where the time goes:
time: 448 us; the launch traced here: 446 us
  waiting for transfers between devices  381 us (85%)
  matrix products  34.9 us (8%)
  between operations  13.1 us (3%)
  other arithmetic  12.7 us (3%)
    reduce_scatter x1, waiting for transfers between devices, body(): lax.psum_scatter(numer, 'ckpt', scatter_dimension=0, tiled=True)  116 us
    reduce_scatter x1, waiting for transfers between devices, body(): lax.psum_scatter(fisher, 'ckpt', scatter_dimension=0, tiled=True)  107 us
    all_gather x1, waiting for transfers between devices, body(): all_rows = lax.all_gather(acts[0], 'tensor', axis=0, tiled=True)  86.7 us
    all_gather x1, waiting for transfers between devices, body(): merged = lax.all_gather(merged_part, 'ckpt', axis=0, tiled=True)  70.5 us
    dot_general x4, matrix products, one_seq(): lax.dot_general(x_rows, g_rows, (((0,), (0,)), ((), ())), preferred_eleme...  34.9 us
  transfers between devices with their start and end apart: 4, of which 4 were waited for; matrix products, arithmetic and copies ran while one was open for 2% of the time, Pallas kernels for 0%

commit v1 on v0

v1 whole, which is shorter than its diff:
```python
import jax
import jax.numpy as jnp
from jax import lax
from jax.experimental import pallas as pl
from jax.experimental.pallas import tpu as pltpu
from jax.sharding import PartitionSpec as P

MESH = pl.DeviceIdType.MESH
F32, BF16, I16, I32 = jnp.float32, jnp.bfloat16, jnp.int16, jnp.int32
UNITS = 14
ROWS = 256
LANES = 128
TILE = 16
SLOTS = 4
D_TOP = 65504.0
D_MID = 32752
R_TOP = 32704.0
W_MAX = 0.125


def fourth_root(v):
    return jnp.sqrt(jnp.sqrt(v))


def wide(tile, count):
    return jnp.concatenate([tile] * count, axis=1)


def scale_of(exponent):
    return jnp.exp2(exponent.astype(F32))


def code_d(v, inverse):
    root = fourth_root(v * inverse)
    code = (root * D_TOP + 0.5).astype(I32) - D_MID
    return jnp.minimum(code, 32767).astype(I16)


def read_d(code, scale):
    root = (code.astype(F32) + float(D_MID)) * (1.0 / D_TOP)
    square = root * root
    return square * square * scale


def code_r(numer, denom):
    mean = numer / jnp.maximum(denom, 1e-30)
    root = fourth_root(jnp.minimum(jnp.abs(mean) * (1.0 / W_MAX), 1.0))
    code = (root * R_TOP + 0.5).astype(I32)
    return jnp.where(mean < 0.0, -code, code).astype(I16)


def read_r(code):
    value = code.astype(F32)
    root = value * (1.0 / R_TOP)
    square = root * root
    return square * square * jnp.where(value < 0.0, -W_MAX, W_MAX)


def kernel(seq_ref, acts_hbm, cot_hbm, w_hbm, out_hbm,
           acts, xt, cot, w_own, w_rx, f32_f, sums, mine, x1s, x1r, x2s, x2r, zs, zr, out,
           load_sem, s_w, r_w, s_one, r_one, s_z, r_z, s_az, r_az, s_out):
    cols = cot.shape[1]
    groups = cols // LANES
    seq_count = seq_ref.shape[0]
    seq_len = cot.shape[0] // seq_count
    ck, tn = lax.axis_index("ckpt"), lax.axis_index("tensor")
    x, zh = ck // 4, ck % 4
    zl, y, core = tn // 8, (tn // 2) % 4, tn % 2
    xa, xb = ((x + 1) // 2) % 2, x // 2
    ya, yb = ((y + 1) // 2) % 2, y // 2
    to_zl = (ck, (1 - zl) * 8 + y * 2 + core)
    to_core = (ck, zl * 8 + y * 2 + 1 - core)
    to_y = [(ck, zl * 8 + (y + 1 - 2 * (y % 2)) * 2 + core), (ck, zl * 8 + (3 - y) * 2 + core)]
    to_x = [((x + 1 - 2 * (x % 2)) * 4 + zh, tn), ((3 - x) * 4 + zh, tn)]
    to_z = [(x * 4 + (zh + j) % 4, tn) for j in range(4)]
    bit = [xa, xb]
    ZL, Y1, Y2, CO, X1, X2, A1, A2 = range(8)

    barrier = pltpu.get_barrier_semaphore()
    others = [to_zl, to_core, *to_y, *to_x, *to_z[1:]]
    for other in others:
        pl.semaphore_signal(barrier, 1, device_id=other, device_id_type=MESH)

    load_acts = pltpu.make_async_copy(acts_hbm, acts, load_sem.at[0])
    load_cot = pltpu.make_async_copy(cot_hbm, cot, load_sem.at[1])
    load_w = pltpu.make_async_copy(w_hbm, w_own, load_sem.at[2])
    load_acts.start()
    load_cot.start()
    load_w.start()

    def rows(n, size):
        return pl.ds(pl.multiple_of(n * size, size), size)

    def remote(src, dst, send, recv, to):
        return pltpu.make_async_remote_copy(src, dst, send, recv, device_id=to, device_id_type=MESH)

    def one(stage, u, ref, to):
        return remote(ref, ref, s_one.at[stage, u], r_one.at[stage, u], to)

    def weights(par):
        return remote(w_hbm.at[:, par, rows(1 - bit[par], ROWS // 2)], w_rx.at[:, par],
                      s_w.at[par], r_w.at[par], to_x[par])

    def copy_zl(u, par):
        return one(ZL, u, xt.at[zl, yb, ya, core, u], to_zl)

    def copy_y1(u, par):
        return one(Y1, u, xt.at[:, yb, ya, core, u], to_y[par])

    def copy_y2(u, par):
        ref = xt.at[:, yb, :, core, u] if par == 0 else xt.at[:, :, ya, core, u]
        return one(Y2, u, ref, to_y[1 - par])

    def copy_core(u, par):
        return one(CO, u, xt.at[:, :, :, core, u], to_core)

    def copy_x1(u, par):
        return remote(x1s.at[u], x1r.at[u], s_one.at[X1, u], r_one.at[X1, u], to_x[par])

    def copy_x2(u, par):
        return remote(x2s.at[u], x2r.at[u], s_one.at[X2, u], r_one.at[X2, u], to_x[1 - par])

    def copy_z(u, j):
        return remote(zs.at[u, j - 1], zr.at[u, j - 1], s_z.at[u, j - 1], r_z.at[u, j - 1], to_z[j])

    def region(u, par, size):
        first, second = bit[par], bit[1 - par]
        if size == 128:
            return out.at[u, rows(first, 128)]
        if size == 64:
            return out.at[u, rows(first * 2 + second, 64)]
        return out.at[u, rows(first * 8 + second * 4 + zh, 16)]

    def copy_az(u, par, j):
        ref = region(u, par, 16)
        return remote(ref, ref, s_az.at[u, j - 1], r_az.at[u, j - 1], to_z[j])

    def copy_a1(u, par):
        return one(A1, u, region(u, par, 64), to_x[1 - par])

    def copy_a2(u, par):
        return one(A2, u, region(u, par, 128), to_x[par])

    def copy_out(u):
        return pltpu.make_async_copy(out.at[u], out_hbm.at[u], s_out.at[u])

    def turn(u):
        block = acts[:, pl.ds(pl.multiple_of(u * ROWS, ROWS), ROWS)]
        xt[zl, yb, ya, core, u] = block.astype(F32).T.astype(BF16)

    def do_turn(u, par):
        turn(u)
        copy_zl(u, par).start()

    def do_y1(u, par):
        copy_zl(u, par).wait_recv()
        copy_y1(u, par).start()

    def do_y2(u, par):
        copy_y1(u, par).wait_recv()
        copy_y2(u, par).start()

    def do_core(u, par):
        copy_y2(u, par).wait_recv()
        copy_core(u, par).start()

    def do_fisher(u, par):
        copy_core(u, par).wait_recv()
        slot = u % SLOTS
        total = None
        for seq in range(seq_count):
            near, far = seq // 2, seq % 2
            order = (0, 1) if far == 0 else (1, 0)
            left = jnp.concatenate(
                [xt[near, far, a, c, u] for a in order for c in range(2)], axis=1)
            grad = jnp.dot(left, cot[seq * seq_len:(seq + 1) * seq_len, :], preferred_element_type=F32)
            total = grad * grad if total is None else total + grad * grad
        f32_f[slot] = total
        most = total[:, :LANES]
        for g in range(1, groups):
            most = jnp.maximum(most, total[:, g * LANES:(g + 1) * LANES])
        top = most[:TILE]
        for r in range(1, ROWS // TILE):
            top = jnp.maximum(top, most[r * TILE:(r + 1) * TILE])
        exponent = jnp.ceil(jnp.log2(jnp.maximum(top, 1e-30)) + 0.01).astype(I32).astype(I16)
        count = ROWS // 2 // TILE
        x1s[u, count * groups] = exponent
        inverse = wide(1.0 / scale_of(exponent), groups)
        base = (1 - bit[par]) * count

        def step(r, carry):
            code = code_d(f32_f[slot, rows(base + r, TILE)], inverse)
            for g in range(groups):
                x1s[u, r * groups + g] = code[:, g * LANES:(g + 1) * LANES]
            return carry

        lax.fori_loop(0, count, step, 0)
        copy_x1(u, par).start()

    def tiles(ref, u, at):
        return jnp.concatenate([ref[u, at + g] for g in range(groups)], axis=1)

    def do_x2(u, par):
        copy_x1(u, par).wait_recv()
        slot = u % SLOTS
        count = ROWS // 2 // TILE
        half = count // 2
        e_own, e_rx = x1s[u, count * groups].astype(I32), x1r[u, count * groups].astype(I32)
        exponent = (jnp.maximum(e_own, e_rx) + 1).astype(I16)
        x2s[u, 2 * half * groups] = exponent
        inverse = wide(1.0 / scale_of(exponent), groups)
        scale = wide(scale_of(e_rx), groups)
        kept = bit[par] * count

        def both(r):
            f_own = f32_f[slot, rows(kept + r, TILE)]
            f_rx = read_d(tiles(x1r, u, r * groups), scale)
            own = w_own[u // 2, par, rows(kept + r, TILE)].astype(F32)
            other = w_rx[u // 2, par, rows(r, TILE)].astype(F32)
            return f_own + f_rx, f_own * own + f_rx * other

        def send(r, carry):
            denom, numer = both((1 - bit[1 - par]) * half + r)
            d, m = code_d(denom, inverse), code_r(numer, denom)
            for g in range(groups):
                x2s[u, r * groups + g] = d[:, g * LANES:(g + 1) * LANES]
                x2s[u, (half + r) * groups + g] = m[:, g * LANES:(g + 1) * LANES]
            return carry

        lax.fori_loop(0, half, send, 0)
        copy_x2(u, par).start()

        def keep(r, carry):
            denom, numer = both(bit[1 - par] * half + r)
            sums[slot, 0, rows(r, TILE)] = denom
            sums[slot, 1, rows(r, TILE)] = numer
            return carry

        lax.fori_loop(0, half, keep, 0)

    def do_z(u, par):
        copy_x2(u, par).wait_recv()
        slot = u % SLOTS
        half = ROWS // 4 // TILE
        e_own, e_rx = x2s[u, 2 * half * groups].astype(I32), x2r[u, 2 * half * groups].astype(I32)
        exponent = (jnp.maximum(e_own, e_rx) + 1).astype(I16)
        inverse = wide(1.0 / scale_of(exponent), groups)
        scale = wide(scale_of(e_rx), groups)
        for j in (1, 2, 3, 0):
            at = (zh + j) % 4
            d_rx = read_d(tiles(x2r, u, at * groups), scale)
            denom = sums[slot, 0, rows(at, TILE)] + d_rx
            numer = sums[slot, 1, rows(at, TILE)] + d_rx * read_r(tiles(x2r, u, (half + at) * groups))
            if j == 0:
                mine[slot, 0] = denom
                mine[slot, 1] = numer
                continue
            d, m = code_d(denom, inverse), code_r(numer, denom)
            for g in range(groups):
                zs[u, j - 1, g] = d[:, g * LANES:(g + 1) * LANES]
                zs[u, j - 1, groups + g] = m[:, g * LANES:(g + 1) * LANES]
            zs[u, j - 1, 2 * groups] = exponent
            copy_z(u, j).start()

    def do_merge(u, par):
        slot = u % SLOTS
        denom, numer = mine[slot, 0], mine[slot, 1]
        for j in (1, 2, 3):
            copy_z(u, j).wait_recv()
            scale = wide(scale_of(zr[u, j - 1, 2 * groups].astype(I32)), groups)
            d_rx = read_d(jnp.concatenate([zr[u, j - 1, g] for g in range(groups)], axis=1), scale)
            m_rx = read_r(jnp.concatenate([zr[u, j - 1, groups + g] for g in range(groups)], axis=1))
            denom = denom + d_rx
            numer = numer + d_rx * m_rx
        region(u, par, 16)[...] = (numer / (denom + 1e-6)).astype(BF16)
        for j in (1, 2, 3):
            copy_az(u, par, j).start()

    def do_a1(u, par):
        for j in (1, 2, 3):
            copy_az(u, par, j).wait_recv()
        copy_a1(u, par).start()

    def do_a2(u, par):
        copy_a1(u, par).wait_recv()
        copy_a2(u, par).start()

    def do_out(u, par):
        copy_a2(u, par).wait_recv()
        copy_out(u).start()

    load_acts.wait()
    pl.semaphore_wait(barrier, len(others))
    for par in range(2):
        weights(par).start()

    load_cot.wait()

    def mask(b, carry):
        size = 64
        seq = b // (seq_len // size)
        at = (b % (seq_len // size)) * size
        block = cot[rows(b, size)].astype(F32)
        position = lax.broadcasted_iota(I32, (size, cols), 0) + at
        cot[rows(b, size)] = jnp.where(position < seq_ref[seq], block, 0.0).astype(BF16)
        return carry

    def prepare(b):
        lax.fori_loop(0, cot.shape[0] // 64, mask, 0)
        load_w.wait()
        for par in range(2):
            weights(par).wait_recv()

    stages = [(do_out, 10), (do_a2, 9), (do_a1, 8), (do_merge, 7), (do_z, 6), (do_x2, 5),
              (do_fisher, 4), (do_core, 3), (do_y2, 2), (do_y1, 1), (do_turn, 0)]

    def pair(p, carry):
        for par in range(2):
            for stage, lag in stages:
                u = p * 2 + (par - lag)
                sort = (par - lag) % 2

                @pl.when(jnp.logical_and(u >= 0, u < UNITS))
                def _(stage=stage, u=u, sort=sort):
                    stage(u, sort)
            if par == 1:
                @pl.when(p == 1)
                def _():
                    prepare(0)
        return carry

    lax.fori_loop(0, (UNITS + 10) // 2, pair, 0)

    for par in range(2):
        weights(par).wait_send()

    def settle(p, carry):
        for par in range(2):
            u = p * 2 + par
            for copy in (copy_zl, copy_y1, copy_y2, copy_core, copy_x1, copy_x2, copy_a1, copy_a2):
                copy(u, par).wait_send()
            for j in (1, 2, 3):
                copy_z(u, j).wait_send()
                copy_az(u, par, j).wait_send()
            copy_out(u).wait()
        return carry

    lax.fori_loop(0, UNITS // 2, settle, 0)


def body(acts, cotangent, seq_lengths, up_weight):
    tokens, cols = cotangent.shape[1:]
    width = acts.shape[2]
    groups = cols // LANES
    any_space = pl.BlockSpec(memory_space=pl.ANY)
    half, quarter = ROWS // 2 // TILE, ROWS // 4 // TILE
    merged = pl.pallas_call(
        kernel,
        out_shape=jax.ShapeDtypeStruct((UNITS, ROWS, cols), BF16),
        in_specs=[pl.BlockSpec(memory_space=pltpu.SMEM), any_space, any_space, any_space],
        out_specs=any_space,
        scratch_shapes=[
            pltpu.VMEM((acts.shape[1], width), BF16),
            pltpu.VMEM((2, 2, 2, 2, UNITS, ROWS, LANES), BF16),
            pltpu.VMEM((tokens, cols), BF16),
            pltpu.VMEM((UNITS // 2, 2, ROWS, cols), BF16),
            pltpu.VMEM((UNITS // 2, 2, ROWS // 2, cols), BF16),
            pltpu.VMEM((SLOTS, ROWS, cols), F32),
            pltpu.VMEM((SLOTS, 2, ROWS // 4, cols), F32),
            pltpu.VMEM((SLOTS, 2, TILE, cols), F32),
            pltpu.VMEM((UNITS, half * groups + 1, TILE, LANES), I16),
            pltpu.VMEM((UNITS, half * groups + 1, TILE, LANES), I16),
            pltpu.VMEM((UNITS, 2 * quarter * groups + 1, TILE, LANES), I16),
            pltpu.VMEM((UNITS, 2 * quarter * groups + 1, TILE, LANES), I16),
            pltpu.VMEM((UNITS, 3, 2 * groups + 1, TILE, LANES), I16),
            pltpu.VMEM((UNITS, 3, 2 * groups + 1, TILE, LANES), I16),
            pltpu.VMEM((UNITS, ROWS, cols), BF16),
            pltpu.SemaphoreType.DMA((3,)),
            pltpu.SemaphoreType.DMA((2,)),
            pltpu.SemaphoreType.DMA((2,)),
            pltpu.SemaphoreType.DMA((8, UNITS)),
            pltpu.SemaphoreType.DMA((8, UNITS)),
            pltpu.SemaphoreType.DMA((UNITS, 3)),
            pltpu.SemaphoreType.DMA((UNITS, 3)),
            pltpu.SemaphoreType.DMA((UNITS, 3)),
            pltpu.SemaphoreType.DMA((UNITS, 3)),
            pltpu.SemaphoreType.DMA((UNITS,)),
        ],
        compiler_params=pltpu.CompilerParams(
            collective_id=0, has_side_effects=True, vmem_limit_bytes=58 * 2**20),
    )(seq_lengths, acts[0], cotangent[0], up_weight[0].reshape(UNITS // 2, 2, ROWS, cols))
    return merged.reshape(width, cols)


def solution(mesh):
    in_specs = (
        P("ckpt", "tensor", None),
        P("ckpt", None, "tensor"),
        P(),
        P("ckpt", None, "tensor"),
    )
    out_specs = P(None, "tensor")
    return jax.shard_map(body, mesh=mesh, in_specs=in_specs, out_specs=out_specs, check_vma=False)
```

time: 448 us -> 168 us (0.38)
  waiting for transfers between devices: 381 us -> 0 us
  Pallas kernels: 0 us -> 162 us
  matrix products: 34.9 us -> 0 us
  between operations: 13.1 us -> 0.01 us
  other arithmetic: 12.7 us -> 0 us
    reduce_scatter x2 -> x0, waiting for transfers between devices: 223 us -> none  [the longest x1 116 us: body(): lax.psum_scatter(numer, 'ckpt', scatter_dimension=0, tiled=True)]
    pallas_call x0 -> x1, Pallas kernels: none -> 162 us  [body(): pl.pallas_call(kernel, out_shape=jax.ShapeDtypeStruct((UNITS, ROWS, cols)...]
    all_gather x2 -> x0, waiting for transfers between devices: 157 us -> none  [the longest x1 86.7 us: body(): all_rows = lax.all_gather(acts[0], 'tensor', axis=0, tiled=True)]
    dot_general x4 -> x0, matrix products: 34.9 us -> none  [one_seq(): lax.dot_general(x_rows, g_rows, (((0,), (0,)), ((), ())), preferred_eleme...]
    mul x1 -> x0, other arithmetic: 8.24 us -> none  [body(): numer = fisher * up_weight[0].astype(jnp.float32)]
  transfers between devices with their start and end apart: 4 -> 0, of which waited for: 4 -> 0; matrix products, arithmetic and copies ran while one was open for 2% -> 0% of each run, Pallas kernels for 0% -> 0%
where the time goes in v1:
time: 168 us; the launch traced here: 166 us
  Pallas kernels  162 us (96%)
  local copies, waits for them, and re-layouts  4.11 us (2%)
    pallas_call x1, Pallas kernels, body(): pl.pallas_call(kernel, out_shape=jax.ShapeDtypeStruct((UNITS, ROWS, cols)...  162 us
    unnamed x1, local copies, waits for them, and re-layouts  4.11 us

profile of v1, /device:TPU:2, one launch (start us, length us, event | category | flops | bytes accessed | tf_op | source)
XLA Modules:
  0.0 166.5 jit_solution(15522872801739738985)
XLA Ops:
  0.0 162.3 %shard_map.46 = bf16[14,256,512]{2,1,0:T(8,128)(2,1)} custom-call(s32[4]{0:T(128)} %seq_ref.1, bf16[128,3584]{1,0:T(8,128)(2,1)} %bitcast.7, bf16[2048,512]{1,0:T(8,128)(2,1)} %bitcast.6, bf16[7,2,256,512]{3,2,1,0:T(8,128)(2,1)} %bitcast.5), custom_call_target="tpu_custom_call" | custom-call | tf_op jit(solution)/shard_map/pallas_call | solution.py:357
  162.3 4.1 %copy.6 = bf16[3584,512]{1,0:T(8,128)(2,1)} copy(bf16[3584,512]{1,0:T(8,128)(2,1)} %bitcast.4) | data formatting | bytes 7340032

commit v2 on v1

--- a/solution.py
+++ b/solution.py
@@ -6,12 +6,24 @@
 from jax.sharding import PartitionSpec as P
 
 MESH = pl.DeviceIdType.MESH
+ORDER = (
+    0, 1, 2, 3, 4, 14, 15, 5, 6, 16, 17, 7, 8, 28, 9, 29,
+    18, 30, 31, 10, 42, 19, 20, 43, 11, 12, 56, 32, 13, 57, 44, 58,
+    70, 45, 21, 33, 71, 34, 59, 72, 84, 22, 46, 85, 73, 60, 35, 47,
+    23, 86, 61, 98, 48, 24, 87, 36, 62, 74, 99, 49, 37, 63, 25, 100,
+    75, 76, 88, 26, 50, 38, 27, 101, 64, 77, 112, 51, 39, 89, 113, 65,
+    114, 90, 115, 40, 52, 102, 66, 41, 103, 78, 126, 53, 91, 67, 104, 79,
+    127, 92, 54, 80, 81, 105, 68, 55, 116, 117, 93, 128, 106, 69, 94, 82,
+    129, 107, 140, 95, 141, 83, 118, 119, 96, 120, 130, 131, 142, 121, 97, 132,
+    108, 143, 109, 133, 144, 110, 134, 135, 145, 111, 122, 123, 146, 147, 124, 125,
+    148, 136, 137, 138, 139, 149, 150, 151, 152, 153,
+)
 F32, BF16, I16, I32 = jnp.float32, jnp.bfloat16, jnp.int16, jnp.int32
 UNITS = 14
 ROWS = 256
 LANES = 128
 TILE = 16
-SLOTS = 4
+SLOTS = 14
 D_TOP = 65504.0
 D_MID = 32752
 R_TOP = 32704.0
@@ -148,6 +160,15 @@
         block = acts[:, pl.ds(pl.multiple_of(u * ROWS, ROWS), ROWS)]
         xt[zl, yb, ya, core, u] = block.astype(F32).T.astype(BF16)
 
+    def mask(b, carry):
+        size = 64
+        seq = b // (seq_len // size)
+        at = (b % (seq_len // size)) * size
+        block = cot[rows(b, size)].astype(F32)
+        position = lax.broadcasted_iota(I32, (size, cols), 0) + at
+        cot[rows(b, size)] = jnp.where(position < seq_ref[seq], block, 0.0).astype(BF16)
+        return carry
+
     def do_turn(u, par):
         turn(u)
         copy_zl(u, par).start()
@@ -166,6 +187,9 @@
 
     def do_fisher(u, par):
         copy_core(u, par).wait_recv()
+        if u == 0:
+            load_cot.wait()
+            lax.fori_loop(0, cot.shape[0] // 64, mask, 0)
         slot = u % SLOTS
         total = None
         for seq in range(seq_count):
@@ -202,6 +226,10 @@
 
     def do_x2(u, par):
         copy_x1(u, par).wait_recv()
+        if u == 0:
+            load_w.wait()
+            for sort in range(2):
+                weights(sort).wait_recv()
         slot = u % SLOTS
         count = ROWS // 2 // TILE
         half = count // 2
@@ -294,42 +322,9 @@
     for par in range(2):
         weights(par).start()
 
-    load_cot.wait()
-
-    def mask(b, carry):
-        size = 64
-        seq = b // (seq_len // size)
-        at = (b % (seq_len // size)) * size
-        block = cot[rows(b, size)].astype(F32)
-        position = lax.broadcasted_iota(I32, (size, cols), 0) + at
-        cot[rows(b, size)] = jnp.where(position < seq_ref[seq], block, 0.0).astype(BF16)
-        return carry
-
-    def prepare(b):
-        lax.fori_loop(0, cot.shape[0] // 64, mask, 0)
-        load_w.wait()
-        for par in range(2):
-            weights(par).wait_recv()
-
-    stages = [(do_out, 10), (do_a2, 9), (do_a1, 8), (do_merge, 7), (do_z, 6), (do_x2, 5),
-              (do_fisher, 4), (do_core, 3), (do_y2, 2), (do_y1, 1), (do_turn, 0)]
-
-    def pair(p, carry):
-        for par in range(2):
-            for stage, lag in stages:
-                u = p * 2 + (par - lag)
-                sort = (par - lag) % 2
-
-                @pl.when(jnp.logical_and(u >= 0, u < UNITS))
-                def _(stage=stage, u=u, sort=sort):
-                    stage(u, sort)
-            if par == 1:
-                @pl.when(p == 1)
-                def _():
-                    prepare(0)
-        return carry
-
-    lax.fori_loop(0, (UNITS + 10) // 2, pair, 0)
+    stages = (do_turn, do_y1, do_y2, do_core, do_fisher, do_x2, do_z, do_merge, do_a1, do_a2, do_out)
+    for step in ORDER:
+        stages[step // UNITS](step % UNITS, step % UNITS % 2)
 
     for par in range(2):
         weights(par).wait_send()

time: 168 us -> 132 us (0.79)
  Pallas kernels: 162 us -> 126 us
    pallas_call x1, Pallas kernels: 162 us -> 126 us  [body(): pl.pallas_call(kernel, out_shape=jax.ShapeDtypeStruct((UNITS, ROWS, cols)...]
where the time goes in v2:
time: 132 us; the launch traced here: 130 us
  Pallas kernels  126 us (95%)
  local copies, waits for them, and re-layouts  4.11 us (3%)
    pallas_call x1, Pallas kernels, body(): pl.pallas_call(kernel, out_shape=jax.ShapeDtypeStruct((UNITS, ROWS, cols)...  126 us
    unnamed x1, local copies, waits for them, and re-layouts  4.11 us

profile of v2, /device:TPU:2, one launch (start us, length us, event | category | flops | bytes accessed | tf_op | source)
XLA Modules:
  0.0 129.7 jit_solution(10739608854807134284)
XLA Ops:
  0.0 125.6 %shard_map.46 = bf16[14,256,512]{2,1,0:T(8,128)(2,1)} custom-call(s32[4]{0:T(128)} %seq_ref.1, bf16[128,3584]{1,0:T(8,128)(2,1)} %bitcast.7, bf16[2048,512]{1,0:T(8,128)(2,1)} %bitcast.6, bf16[7,2,256,512]{3,2,1,0:T(8,128)(2,1)} %bitcast.5), custom_call_target="tpu_custom_call" | custom-call | tf_op jit(solution)/shard_map/pallas_call | solution.py:352
  125.6 4.1 %copy.6 = bf16[3584,512]{1,0:T(8,128)(2,1)} copy(bf16[3584,512]{1,0:T(8,128)(2,1)} %bitcast.4) | data formatting | bytes 7340032

commit v3 on v2

--- a/solution.py
+++ b/solution.py
@@ -6,17 +6,23 @@
 from jax.sharding import PartitionSpec as P
 
 MESH = pl.DeviceIdType.MESH
+LATE_ZL = (0,)
+TREE_Z = (0, 1, 2, 3, 4, 5, 6, 7, 8, 9)
+TREE_B = ()
+DIRECT_X = (12, 13)
 ORDER = (
-    0, 1, 2, 3, 4, 14, 15, 5, 6, 16, 17, 7, 8, 28, 9, 29,
-    18, 30, 31, 10, 42, 19, 20, 43, 11, 12, 56, 32, 13, 57, 44, 58,
-    70, 45, 21, 33, 71, 34, 59, 72, 84, 22, 46, 85, 73, 60, 35, 47,
-    23, 86, 61, 98, 48, 24, 87, 36, 62, 74, 99, 49, 37, 63, 25, 100,
-    75, 76, 88, 26, 50, 38, 27, 101, 64, 77, 112, 51, 39, 89, 113, 65,
-    114, 90, 115, 40, 52, 102, 66, 41, 103, 78, 126, 53, 91, 67, 104, 79,
-    127, 92, 54, 80, 81, 105, 68, 55, 116, 117, 93, 128, 106, 69, 94, 82,
-    129, 107, 140, 95, 141, 83, 118, 119, 96, 120, 130, 131, 142, 121, 97, 132,
-    108, 143, 109, 133, 144, 110, 134, 135, 145, 111, 122, 123, 146, 147, 124, 125,
-    148, 136, 137, 138, 139, 149, 150, 151, 152, 153,
+    0, 1, 2, 3, 4, 5, 14, 6, 15, 16, 17, 18, 28, 7, 8, 19,
+    29, 30, 31, 42, 32, 20, 43, 21, 56, 57, 9, 33, 22, 44, 58, 70,
+    45, 23, 71, 46, 34, 35, 10, 59, 11, 60, 72, 84, 47, 24, 36, 85,
+    73, 37, 12, 61, 25, 13, 48, 86, 98, 74, 62, 49, 87, 75, 99, 63,
+    112, 100, 126, 50, 88, 38, 76, 113, 64, 39, 89, 51, 140, 127, 101, 77,
+    114, 128, 26, 65, 102, 90, 78, 154, 27, 52, 115, 91, 66, 103, 53, 79,
+    40, 41, 129, 141, 142, 168, 104, 116, 67, 92, 117, 80, 143, 118, 93, 81,
+    130, 144, 105, 54, 106, 155, 131, 156, 94, 157, 55, 132, 68, 107, 69, 119,
+    145, 169, 95, 158, 120, 170, 133, 108, 134, 171, 121, 109, 135, 146, 82, 147,
+    83, 159, 160, 122, 172, 123, 136, 96, 148, 161, 149, 173, 97, 150, 137, 151,
+    110, 162, 174, 111, 163, 175, 124, 138, 164, 165, 125, 176, 139, 177, 152, 178,
+    179, 166, 153, 167, 180, 181,
 )
 F32, BF16, I16, I32 = jnp.float32, jnp.bfloat16, jnp.int16, jnp.int32
 UNITS = 14
@@ -69,8 +75,9 @@
 
 
 def kernel(seq_ref, acts_hbm, cot_hbm, w_hbm, out_hbm,
-           acts, xt, cot, w_own, w_rx, f32_f, sums, mine, x1s, x1r, x2s, x2r, zs, zr, out,
-           load_sem, s_w, r_w, s_one, r_one, s_z, r_z, s_az, r_az, s_out):
+           acts, xt, cot, w_own, w_rx, f32_f, sums, sums2, mine,
+           x1s, x1r, x2s, x2r, zas, zar, zs, zr, out,
+           load_sem, s_w, r_w, s_one, r_one, s_z, r_z, s_az, r_az, s_ad, r_ad, s_out):
     cols = cot.shape[1]
     groups = cols // LANES
     seq_count = seq_ref.shape[0]
@@ -84,12 +91,23 @@
     to_core = (ck, zl * 8 + y * 2 + 1 - core)
     to_y = [(ck, zl * 8 + (y + 1 - 2 * (y % 2)) * 2 + core), (ck, zl * 8 + (3 - y) * 2 + core)]
     to_x = [((x + 1 - 2 * (x % 2)) * 4 + zh, tn), ((3 - x) * 4 + zh, tn)]
+    to_far_x = ((x + 2) % 4 * 4 + zh, tn)
     to_z = [(x * 4 + (zh + j) % 4, tn) for j in range(4)]
+    to_zp = [(x * 4 + zh + 1 - 2 * (zh % 2), tn), (x * 4 + 3 - zh, tn)]
     bit = [xa, xb]
-    ZL, Y1, Y2, CO, X1, X2, A1, A2 = range(8)
+
+    def z_bits(n):
+        return [((n + 1) // 2) % 2, n // 2]
+
+    def group(n, par):
+        bits = z_bits(n)
+        return bits[par] * 2 + bits[1 - par]
+
+    z_bit = z_bits(zh)
+    ZL, Y0, Y1, Y2, CO, X1, X2, ZA, B1, B2, A1, A2 = range(12)
 
     barrier = pltpu.get_barrier_semaphore()
-    others = [to_zl, to_core, *to_y, *to_x, *to_z[1:]]
+    others = [to_zl, to_core, *to_y, *to_x, to_far_x, *to_z[1:]]
     for other in others:
         pl.semaphore_signal(barrier, 1, device_id=other, device_id_type=MESH)
 
@@ -114,13 +132,18 @@
                       s_w.at[par], r_w.at[par], to_x[par])
 
     def copy_zl(u, par):
-        return one(ZL, u, xt.at[zl, yb, ya, core, u], to_zl)
+        ref = xt.at[zl, :, :, core, u] if u in LATE_ZL else xt.at[zl, yb, ya, core, u]
+        return one(ZL, u, ref, to_zl)
+
+    def copy_y0(u, par):
+        return one(Y0, u, xt.at[zl, yb, ya, core, u], to_y[par])
 
     def copy_y1(u, par):
-        return one(Y1, u, xt.at[:, yb, ya, core, u], to_y[par])
+        return one(Y1, u, xt.at[1 - zl, yb, ya, core, u], to_y[par])
 
     def copy_y2(u, par):
-        ref = xt.at[:, yb, :, core, u] if par == 0 else xt.at[:, :, ya, core, u]
+        layer = zl if u in LATE_ZL else slice(None)
+        ref = xt.at[layer, yb, :, core, u] if par == 0 else xt.at[layer, :, ya, core, u]
         return one(Y2, u, ref, to_y[1 - par])
 
     def copy_core(u, par):
@@ -141,7 +164,26 @@
             return out.at[u, rows(first, 128)]
         if size == 64:
             return out.at[u, rows(first * 2 + second, 64)]
-        return out.at[u, rows(first * 8 + second * 4 + zh, 16)]
+        if size == 32:
+            return out.at[u, rows(first * 4 + second * 2 + z_bit[par], 32)]
+        return out.at[u, rows(first * 8 + second * 4 + group(zh, par), 16)]
+
+    def copy_za(u, par):
+        return remote(zas.at[u], zar.at[u], s_one.at[ZA, u], r_one.at[ZA, u], to_zp[par])
+
+    def copy_zb(u, par):
+        return remote(zs.at[u, 0], zr.at[u, 0], s_z.at[u, 0], r_z.at[u, 0], to_zp[1 - par])
+
+    def copy_b1(u, par):
+        return one(B1, u, region(u, par, 16), to_zp[1 - par])
+
+    def copy_b2(u, par):
+        return one(B2, u, region(u, par, 32), to_zp[par])
+
+    def copies_ad(u, par):
+        ref = region(u, par, 64)
+        return [remote(ref, ref, s_ad.at[u, k], r_ad.at[u, k], to)
+                for k, to in enumerate((*to_x, to_far_x))]
 
     def copy_az(u, par, j):
         ref = region(u, par, 16)
@@ -171,18 +213,29 @@
 
     def do_turn(u, par):
         turn(u)
-        copy_zl(u, par).start()
+        if u not in LATE_ZL:
+            copy_zl(u, par).start()
+        copy_y0(u, par).start()
 
     def do_y1(u, par):
-        copy_zl(u, par).wait_recv()
-        copy_y1(u, par).start()
+        if u in LATE_ZL:
+            copy_y0(u, par).wait_recv()
+            copy_y2(u, par).start()
+        else:
+            copy_zl(u, par).wait_recv()
+            copy_y1(u, par).start()
 
     def do_y2(u, par):
-        copy_y1(u, par).wait_recv()
-        copy_y2(u, par).start()
+        if u in LATE_ZL:
+            copy_y2(u, par).wait_recv()
+            copy_zl(u, par).start()
+        else:
+            copy_y0(u, par).wait_recv()
+            copy_y1(u, par).wait_recv()
+            copy_y2(u, par).start()
 
     def do_core(u, par):
-        copy_y2(u, par).wait_recv()
+        (copy_zl if u in LATE_ZL else copy_y2)(u, par).wait_recv()
         copy_core(u, par).start()
 
     def do_fisher(u, par):
@@ -266,6 +319,10 @@
 
         lax.fori_loop(0, half, keep, 0)
 
+    def put(ref, at, code):
+        for g in range(groups):
+            ref[at + g] = code[:, g * LANES:(g + 1) * LANES]
+
     def do_z(u, par):
         copy_x2(u, par).wait_recv()
         slot = u % SLOTS
@@ -274,47 +331,104 @@
         exponent = (jnp.maximum(e_own, e_rx) + 1).astype(I16)
         inverse = wide(1.0 / scale_of(exponent), groups)
         scale = wide(scale_of(e_rx), groups)
-        for j in (1, 2, 3, 0):
-            at = (zh + j) % 4
+
+        def four(at):
             d_rx = read_d(tiles(x2r, u, at * groups), scale)
-            denom = sums[slot, 0, rows(at, TILE)] + d_rx
-            numer = sums[slot, 1, rows(at, TILE)] + d_rx * read_r(tiles(x2r, u, (half + at) * groups))
+            m_rx = read_r(tiles(x2r, u, (half + at) * groups))
+            return sums[slot, 0, rows(at, TILE)] + d_rx, sums[slot, 1, rows(at, TILE)] + d_rx * m_rx
+
+        if u in TREE_Z:
+            for n in range(2):
+                denom, numer = four((1 - z_bit[par]) * 2 + n)
+                put(zas.at[u], n * groups, code_d(denom, inverse))
+                put(zas.at[u], (2 + n) * groups, code_r(numer, denom))
+            zas[u, 4 * groups] = exponent
+            copy_za(u, par).start()
+            for n in range(2):
+                denom, numer = four(z_bit[par] * 2 + n)
+                sums2[slot, 0, n * TILE:(n + 1) * TILE] = denom
+                sums2[slot, 1, n * TILE:(n + 1) * TILE] = numer
+            return
+        for j in (2, 1, 3, 0):
+            denom, numer = four(group((zh + j) % 4, par))
             if j == 0:
                 mine[slot, 0] = denom
                 mine[slot, 1] = numer
                 continue
-            d, m = code_d(denom, inverse), code_r(numer, denom)
-            for g in range(groups):
-                zs[u, j - 1, g] = d[:, g * LANES:(g + 1) * LANES]
-                zs[u, j - 1, groups + g] = m[:, g * LANES:(g + 1) * LANES]
+            put(zs.at[u, j - 1], 0, code_d(denom, inverse))
+            put(zs.at[u, j - 1], groups, code_r(numer, denom))
             zs[u, j - 1, 2 * groups] = exponent
             copy_z(u, j).start()
+
+    def do_zz(u, par):
+        if u not in TREE_Z:
+            return
+        copy_za(u, par).wait_recv()
+        slot = u % SLOTS
+        e_own, e_rx = zas[u, 4 * groups].astype(I32), zar[u, 4 * groups].astype(I32)
+        exponent = (jnp.maximum(e_own, e_rx) + 1).astype(I16)
+        inverse = wide(1.0 / scale_of(exponent), groups)
+        scale = wide(scale_of(e_rx), groups)
+
+        def eight(at):
+            d_rx = read_d(tiles(zar, u, at * groups), scale)
+            m_rx = read_r(tiles(zar, u, (2 + at) * groups))
+            return sums2[slot, 0, rows(at, TILE)] + d_rx, sums2[slot, 1, rows(at, TILE)] + d_rx * m_rx
+
+        denom, numer = eight(1 - z_bit[1 - par])
+        put(zs.at[u, 0], 0, code_d(denom, inverse))
+        put(zs.at[u, 0], groups, code_r(numer, denom))
+        zs[u, 0, 2 * groups] = exponent
+        copy_zb(u, par).start()
+        denom, numer = eight(z_bit[1 - par])
+        mine[slot, 0] = denom
+        mine[slot, 1] = numer
 
     def do_merge(u, par):
         slot = u % SLOTS
         denom, numer = mine[slot, 0], mine[slot, 1]
-        for j in (1, 2, 3):
-            copy_z(u, j).wait_recv()
+        for j in (1,) if u in TREE_Z else (1, 2, 3):
+            (copy_zb(u, par) if u in TREE_Z else copy_z(u, j)).wait_recv()
             scale = wide(scale_of(zr[u, j - 1, 2 * groups].astype(I32)), groups)
             d_rx = read_d(jnp.concatenate([zr[u, j - 1, g] for g in range(groups)], axis=1), scale)
             m_rx = read_r(jnp.concatenate([zr[u, j - 1, groups + g] for g in range(groups)], axis=1))
             denom = denom + d_rx
             numer = numer + d_rx * m_rx
         region(u, par, 16)[...] = (numer / (denom + 1e-6)).astype(BF16)
-        for j in (1, 2, 3):
-            copy_az(u, par, j).start()
+        if u in TREE_B:
+            copy_b1(u, par).start()
+        else:
+            for j in (2, 1, 3):
+                copy_az(u, par, j).start()
+
+    def do_b2(u, par):
+        if u in TREE_B:
+            copy_b1(u, par).wait_recv()
+            copy_b2(u, par).start()
 
     def do_a1(u, par):
-        for j in (1, 2, 3):
-            copy_az(u, par, j).wait_recv()
-        copy_a1(u, par).start()
+        if u in TREE_B:
+            copy_b2(u, par).wait_recv()
+        else:
+            for j in (1, 2, 3):
+                copy_az(u, par, j).wait_recv()
+        if u in DIRECT_X:
+            for copy in copies_ad(u, par):
+                copy.start()
+        else:
+            copy_a1(u, par).start()
 
     def do_a2(u, par):
-        copy_a1(u, par).wait_recv()
-        copy_a2(u, par).start()
+        if u not in DIRECT_X:
+            copy_a1(u, par).wait_recv()
+            copy_a2(u, par).start()
 
     def do_out(u, par):
-        copy_a2(u, par).wait_recv()
+        if u in DIRECT_X:
+            for copy in copies_ad(u, par):
+                copy.wait_recv()
+        else:
+            copy_a2(u, par).wait_recv()
         copy_out(u).start()
 
     load_acts.wait()
@@ -322,25 +436,26 @@
     for par in range(2):
         weights(par).start()
 
-    stages = (do_turn, do_y1, do_y2, do_core, do_fisher, do_x2, do_z, do_merge, do_a1, do_a2, do_out)
+    stages = (do_turn, do_y1, do_y2, do_core, do_fisher, do_x2, do_z, do_zz, do_merge,
+              do_b2, do_a1, do_a2, do_out)
     for step in ORDER:
         stages[step // UNITS](step % UNITS, step % UNITS % 2)
 
     for par in range(2):
         weights(par).wait_send()
 
-    def settle(p, carry):
-        for par in range(2):
-            u = p * 2 + par
-            for copy in (copy_zl, copy_y1, copy_y2, copy_core, copy_x1, copy_x2, copy_a1, copy_a2):
-                copy(u, par).wait_send()
-            for j in (1, 2, 3):
-                copy_z(u, j).wait_send()
-                copy_az(u, par, j).wait_send()
-            copy_out(u).wait()
-        return carry
-
-    lax.fori_loop(0, UNITS // 2, settle, 0)
+    for u in range(UNITS):
+        par = u % 2
+        sent = [copy_zl(u, par), copy_y0(u, par), copy_y2(u, par), copy_core(u, par),
+                copy_x1(u, par), copy_x2(u, par)]
+        if u not in LATE_ZL:
+            sent.append(copy_y1(u, par))
+        sent += [copy_za(u, par), copy_zb(u, par)] if u in TREE_Z else [copy_z(u, j) for j in (1, 2, 3)]
+        sent += [copy_b1(u, par), copy_b2(u, par)] if u in TREE_B else [copy_az(u, par, j) for j in (1, 2, 3)]
+        sent += copies_ad(u, par) if u in DIRECT_X else [copy_a1(u, par), copy_a2(u, par)]
+        for copy in sent:
+            copy.wait_send()
+        copy_out(u).wait()
 
 
 def body(acts, cotangent, seq_lengths, up_weight):
@@ -362,19 +477,24 @@
             pltpu.VMEM((UNITS // 2, 2, ROWS // 2, cols), BF16),
             pltpu.VMEM((SLOTS, ROWS, cols), F32),
             pltpu.VMEM((SLOTS, 2, ROWS // 4, cols), F32),
+            pltpu.VMEM((SLOTS, 2, 2 * TILE, cols), F32),
             pltpu.VMEM((SLOTS, 2, TILE, cols), F32),
             pltpu.VMEM((UNITS, half * groups + 1, TILE, LANES), I16),
             pltpu.VMEM((UNITS, half * groups + 1, TILE, LANES), I16),
             pltpu.VMEM((UNITS, 2 * quarter * groups + 1, TILE, LANES), I16),
             pltpu.VMEM((UNITS, 2 * quarter * groups + 1, TILE, LANES), I16),
+            pltpu.VMEM((UNITS, 4 * groups + 1, TILE, LANES), I16),
+            pltpu.VMEM((UNITS, 4 * groups + 1, TILE, LANES), I16),
             pltpu.VMEM((UNITS, 3, 2 * groups + 1, TILE, LANES), I16),
             pltpu.VMEM((UNITS, 3, 2 * groups + 1, TILE, LANES), I16),
             pltpu.VMEM((UNITS, ROWS, cols), BF16),
             pltpu.SemaphoreType.DMA((3,)),
             pltpu.SemaphoreType.DMA((2,)),
             pltpu.SemaphoreType.DMA((2,)),
-            pltpu.SemaphoreType.DMA((8, UNITS)),
-            pltpu.SemaphoreType.DMA((8, UNITS)),
+            pltpu.SemaphoreType.DMA((12, UNITS)),
+            pltpu.SemaphoreType.DMA((12, UNITS)),
+            pltpu.SemaphoreType.DMA((UNITS, 3)),
+            pltpu.SemaphoreType.DMA((UNITS, 3)),
             pltpu.SemaphoreType.DMA((UNITS, 3)),
             pltpu.SemaphoreType.DMA((UNITS, 3)),
             pltpu.SemaphoreType.DMA((UNITS, 3)),

time: 132 us -> 126 us (0.955); the launches traced: 130 us -> 126 us
  Pallas kernels: 126 us -> 122 us
    pallas_call x1, Pallas kernels: 126 us -> 122 us  [body(): pl.pallas_call(kernel, out_shape=jax.ShapeDtypeStruct((UNITS, ROWS, cols)...]
where the time goes in v3:
time: 126 us
  Pallas kernels  122 us (97%)
  local copies, waits for them, and re-layouts  4.11 us (3%)
    pallas_call x1, Pallas kernels, body(): pl.pallas_call(kernel, out_shape=jax.ShapeDtypeStruct((UNITS, ROWS, cols)...  122 us
    unnamed x1, local copies, waits for them, and re-layouts  4.11 us

profile of v3, /device:TPU:2, one launch (start us, length us, event | category | flops | bytes accessed | tf_op | source)
XLA Modules:
  0.0 126.2 jit_solution(5653664126414393624)
XLA Ops:
  0.0 122.1 %shard_map.46 = bf16[14,256,512]{2,1,0:T(8,128)(2,1)} custom-call(s32[4]{0:T(128)} %seq_ref.1, bf16[128,3584]{1,0:T(8,128)(2,1)} %bitcast.7, bf16[2048,512]{1,0:T(8,128)(2,1)} %bitcast.6, bf16[7,2,256,512]{3,2,1,0:T(8,128)(2,1)} %bitcast.5), custom_call_target="tpu_custom_call" | custom-call | tf_op jit(solution)/shard_map/pallas_call | solution.py:467
  122.1 4.1 %copy.6 = bf16[3584,512]{1,0:T(8,128)(2,1)} copy(bf16[3584,512]{1,0:T(8,128)(2,1)} %bitcast.4) | data formatting | bytes 7340032

commit v4 on v3

--- a/solution.py
+++ b/solution.py
@@ -74,10 +74,10 @@
     return square * square * jnp.where(value < 0.0, -W_MAX, W_MAX)
 
 
-def kernel(seq_ref, acts_hbm, cot_hbm, w_hbm, out_hbm,
+def kernel(seq_ref, acts_hbm, cot_hbm, w_hbm, out,
            acts, xt, cot, w_own, w_rx, f32_f, sums, sums2, mine,
-           x1s, x1r, x2s, x2r, zas, zar, zs, zr, out,
-           load_sem, s_w, r_w, s_one, r_one, s_z, r_z, s_az, r_az, s_ad, r_ad, s_out):
+           x1s, x1r, x2s, x2r, zas, zar, zs, zr,
+           load_sem, s_w, r_w, s_one, r_one, s_z, r_z, s_az, r_az, s_ad, r_ad):
     cols = cot.shape[1]
     groups = cols // LANES
     seq_count = seq_ref.shape[0]
@@ -194,9 +194,6 @@
 
     def copy_a2(u, par):
         return one(A2, u, region(u, par, 128), to_x[par])
-
-    def copy_out(u):
-        return pltpu.make_async_copy(out.at[u], out_hbm.at[u], s_out.at[u])
 
     def turn(u):
         block = acts[:, pl.ds(pl.multiple_of(u * ROWS, ROWS), ROWS)]
@@ -429,7 +426,6 @@
                 copy.wait_recv()
         else:
             copy_a2(u, par).wait_recv()
-        copy_out(u).start()
 
     load_acts.wait()
     pl.semaphore_wait(barrier, len(others))
@@ -455,7 +451,6 @@
         sent += copies_ad(u, par) if u in DIRECT_X else [copy_a1(u, par), copy_a2(u, par)]
         for copy in sent:
             copy.wait_send()
-        copy_out(u).wait()
 
 
 def body(acts, cotangent, seq_lengths, up_weight):
@@ -466,9 +461,9 @@
     half, quarter = ROWS // 2 // TILE, ROWS // 4 // TILE
     merged = pl.pallas_call(
         kernel,
-        out_shape=jax.ShapeDtypeStruct((UNITS, ROWS, cols), BF16),
+        out_shape=pltpu.VMEM((UNITS, ROWS, cols), BF16),
         in_specs=[pl.BlockSpec(memory_space=pltpu.SMEM), any_space, any_space, any_space],
-        out_specs=any_space,
+        out_specs=pl.BlockSpec(memory_space=pltpu.VMEM),
         scratch_shapes=[
             pltpu.VMEM((acts.shape[1], width), BF16),
             pltpu.VMEM((2, 2, 2, 2, UNITS, ROWS, LANES), BF16),
@@ -487,7 +482,6 @@
             pltpu.VMEM((UNITS, 4 * groups + 1, TILE, LANES), I16),
             pltpu.VMEM((UNITS, 3, 2 * groups + 1, TILE, LANES), I16),
             pltpu.VMEM((UNITS, 3, 2 * groups + 1, TILE, LANES), I16),
-            pltpu.VMEM((UNITS, ROWS, cols), BF16),
             pltpu.SemaphoreType.DMA((3,)),
             pltpu.SemaphoreType.DMA((2,)),
             pltpu.SemaphoreType.DMA((2,)),
@@ -499,10 +493,9 @@
             pltpu.SemaphoreType.DMA((UNITS, 3)),
             pltpu.SemaphoreType.DMA((UNITS, 3)),
             pltpu.SemaphoreType.DMA((UNITS, 3)),
-            pltpu.SemaphoreType.DMA((UNITS,)),
         ],
         compiler_params=pltpu.CompilerParams(
-            collective_id=0, has_side_effects=True, vmem_limit_bytes=58 * 2**20),
+            collective_id=0, has_side_effects=True, vmem_limit_bytes=54 * 2**20),
     )(seq_lengths, acts[0], cotangent[0], up_weight[0].reshape(UNITS // 2, 2, ROWS, cols))
     return merged.reshape(width, cols)
 

time: 126 us -> 123 us (0.976)
  local copies, waits for them, and re-layouts: 4.11 us -> 1.84 us
    unnamed x1, local copies, waits for them, and re-layouts: 4.11 us -> 1.84 us
where the time goes in v4:
time: 123 us
  Pallas kernels  122 us (99%)
  local copies, waits for them, and re-layouts  1.84 us (1%)
    pallas_call x1, Pallas kernels, body(): pl.pallas_call(kernel, out_shape=pltpu.VMEM((UNITS, ROWS, cols), BF16), i...  122 us

profile of v4, /device:TPU:2, one launch (start us, length us, event | category | flops | bytes accessed | tf_op | source)
XLA Modules:
  0.0 123.4 jit_solution(15008634388179580908)
XLA Ops:
  0.0 121.6 %shard_map.46 = bf16[14,256,512]{2,1,0:T(8,128)(2,1)S(1)} custom-call(s32[4]{0:T(128)} %seq_ref.1, bf16[128,3584]{1,0:T(8,128)(2,1)} %bitcast.7, bf16[2048,512]{1,0:T(8,128)(2,1)} %bitcast.6, bf16[7,2,256,512]{3,2,1,0:T(8,128)(2,1)} %bitcast.5), custom_call_target="tpu_custom_call" | custom-call | tf_op jit(solution)/shard_map/pallas_call | solution.py:462
  121.6 1.8 %copy.6 = bf16[3584,512]{1,0:T(8,128)(2,1)} copy(bf16[3584,512]{1,0:T(8,128)(2,1)S(1)} %bitcast.4) | data formatting | bytes 7340032

commit v5 on v4

--- a/solution.py
+++ b/solution.py
@@ -6,23 +6,24 @@
 from jax.sharding import PartitionSpec as P
 
 MESH = pl.DeviceIdType.MESH
-LATE_ZL = (0,)
-TREE_Z = (0, 1, 2, 3, 4, 5, 6, 7, 8, 9)
+LATE_ZL = (0, 3)
+TREE_Z = (0, 1, 2, 3, 4, 5, 6, 7, 8, 9, 10, 11)
 TREE_B = ()
 DIRECT_X = (12, 13)
+TURNED = 4
 ORDER = (
-    0, 1, 2, 3, 4, 5, 14, 6, 15, 16, 17, 18, 28, 7, 8, 19,
-    29, 30, 31, 42, 32, 20, 43, 21, 56, 57, 9, 33, 22, 44, 58, 70,
-    45, 23, 71, 46, 34, 35, 10, 59, 11, 60, 72, 84, 47, 24, 36, 85,
-    73, 37, 12, 61, 25, 13, 48, 86, 98, 74, 62, 49, 87, 75, 99, 63,
-    112, 100, 126, 50, 88, 38, 76, 113, 64, 39, 89, 51, 140, 127, 101, 77,
-    114, 128, 26, 65, 102, 90, 78, 154, 27, 52, 115, 91, 66, 103, 53, 79,
-    40, 41, 129, 141, 142, 168, 104, 116, 67, 92, 117, 80, 143, 118, 93, 81,
-    130, 144, 105, 54, 106, 155, 131, 156, 94, 157, 55, 132, 68, 107, 69, 119,
-    145, 169, 95, 158, 120, 170, 133, 108, 134, 171, 121, 109, 135, 146, 82, 147,
-    83, 159, 160, 122, 172, 123, 136, 96, 148, 161, 149, 173, 97, 150, 137, 151,
-    110, 162, 174, 111, 163, 175, 124, 138, 164, 165, 125, 176, 139, 177, 152, 178,
-    179, 166, 153, 167, 180, 181,
+    0, 1, 2, 3, 4, 5, 14, 6, 15, 16, 17, 7, 18, 19, 28, 29,
+    20, 21, 8, 30, 31, 42, 9, 22, 43, 32, 56, 33, 34, 57, 44, 58,
+    45, 35, 10, 70, 71, 23, 46, 36, 59, 60, 11, 47, 24, 72, 84, 85,
+    48, 61, 73, 25, 37, 12, 62, 86, 74, 49, 38, 98, 26, 99, 87, 63,
+    50, 75, 13, 112, 76, 64, 39, 51, 113, 100, 27, 88, 77, 65, 126, 89,
+    101, 52, 90, 140, 78, 127, 40, 141, 114, 66, 53, 41, 102, 91, 79, 67,
+    128, 115, 129, 103, 154, 80, 155, 54, 104, 116, 92, 130, 142, 81, 55, 93,
+    143, 117, 168, 68, 94, 144, 69, 105, 95, 169, 156, 106, 107, 131, 157, 158,
+    82, 118, 108, 119, 132, 109, 145, 83, 170, 120, 171, 146, 133, 121, 134, 135,
+    172, 159, 122, 147, 160, 123, 136, 96, 148, 137, 149, 161, 173, 150, 97, 151,
+    110, 174, 162, 163, 124, 111, 175, 164, 165, 125, 176, 138, 152, 177, 166, 178,
+    179, 139, 153, 180, 167, 181,
 )
 F32, BF16, I16, I32 = jnp.float32, jnp.bfloat16, jnp.int16, jnp.int32
 UNITS = 14
@@ -209,12 +210,16 @@
         return carry
 
     def do_turn(u, par):
-        turn(u)
+        if u >= TURNED:
+            turn(u)
         if u not in LATE_ZL:
             copy_zl(u, par).start()
         copy_y0(u, par).start()
 
     def do_y1(u, par):
+        if u == 0:
+            load_cot.wait()
+            lax.fori_loop(0, cot.shape[0] // 64, mask, 0)
         if u in LATE_ZL:
             copy_y0(u, par).wait_recv()
             copy_y2(u, par).start()
@@ -237,9 +242,6 @@
 
     def do_fisher(u, par):
         copy_core(u, par).wait_recv()
-        if u == 0:
-            load_cot.wait()
-            lax.fori_loop(0, cot.shape[0] // 64, mask, 0)
         slot = u % SLOTS
         total = None
         for seq in range(seq_count):
@@ -428,6 +430,8 @@
             copy_a2(u, par).wait_recv()
 
     load_acts.wait()
+    for u in range(TURNED):
+        turn(u)
     pl.semaphore_wait(barrier, len(others))
     for par in range(2):
         weights(par).start()

time: 123 us -> 121 us (0.984)
  Pallas kernels: 122 us -> 118 us
    pallas_call x1, Pallas kernels: 122 us -> 118 us  [body(): pl.pallas_call(kernel, out_shape=pltpu.VMEM((UNITS, ROWS, cols), BF16), i...]
where the time goes in v5:
time: 121 us; the launch traced here: 120 us
  Pallas kernels  118 us (98%)
  local copies, waits for them, and re-layouts  1.84 us (2%)
    pallas_call x1, Pallas kernels, body(): pl.pallas_call(kernel, out_shape=pltpu.VMEM((UNITS, ROWS, cols), BF16), i...  118 us

profile of v5, /device:TPU:2, one launch (start us, length us, event | category | flops | bytes accessed | tf_op | source)
XLA Modules:
  0.0 120.3 jit_solution(4787311140741692952)
XLA Ops:
  0.0 118.4 %shard_map.46 = bf16[14,256,512]{2,1,0:T(8,128)(2,1)S(1)} custom-call(s32[4]{0:T(128)} %seq_ref.1, bf16[128,3584]{1,0:T(8,128)(2,1)} %bitcast.7, bf16[2048,512]{1,0:T(8,128)(2,1)} %bitcast.6, bf16[7,2,256,512]{3,2,1,0:T(8,128)(2,1)} %bitcast.5), custom_call_target="tpu_custom_call" | custom-call | tf_op jit(solution)/shard_map/pallas_call | solution.py:466
  118.4 1.8 %copy.6 = bf16[3584,512]{1,0:T(8,128)(2,1)} copy(bf16[3584,512]{1,0:T(8,128)(2,1)S(1)} %bitcast.4) | data formatting | bytes 7340032
